TPU v7x, 512 devices: a whole 4x4x16 slice. The times are simulated.
512 devices in a mesh: feat: 16 (over z), batch: 32 (over y, x, core).
Axes of the slice: x: 4, y: 4, z: 16, core: 2. Of those that a mesh axis runs over, the one named last changes fastest.
Arguments:
- feats: bfloat16 [32, 768, 8192], P('batch', 'feat'), may hold values from -6 to 6
- nbr_one: int32 [32, 15, 1024], P('batch'), may hold values from 0 to 8191
- rel_one: int32 [32, 15, 1024], P('batch'), may hold values from 0 to 4
- w_one: bfloat16 [5, 768, 1024], P(None, 'feat'), may hold values from -0.09375 to 0.09375
- owner_two: int32 [32, 1024, 10, 1], P('batch'), may hold values from 0 to 31; in each aligned block of 640 rows (0 to 639, 640 to 1279, ..., all dimensions but the last counted through in order) at most 40 rows name the same one
- local_two: int32 [32, 1024, 10], P('batch'), may hold values from 0 to 63
- rel_two: int32 [32, 1024, 10], P('batch'), may hold values from 0 to 4
- w_two: bfloat16 [5, 1024, 1024], P(None, 'feat'), may hold values from -0.078125 to 0.078125
Outputs:
- hidden_two: bfloat16 [32, 1024, 1024], P('batch', 'feat')
Inputs may be any that keep to these rules, and one draw needn't show every extreme that they name: `owner_two`: every neighbour of destination j lies in the block of rows (j // 64) * 64 to (j // 64) * 64 + 63 of its mini-batch; among the 640 edges of each aligned block of 64 destinations, no mini-batch is named more than 40 times. `rel_one`: the value 4 marks an empty slot. `rel_two`: the value 4 marks an empty slot.
All inputs are finite; a program needn't handle non-finite values.
Results may differ from a plain program's by a relative error of at most 0.025.
Values may be sent and summed in bfloat16 or wider, within the bound.
A program may use at most 64 MiB of HBM per device.

v0:
```python
import jax
import jax.numpy as jnp
from jax import lax
from jax.sharding import PartitionSpec as P

RELATIONS = 4
FANOUT_TWO = 10
ROWS = 64


def relation_counts(relation_ids, along):
    counted = [
        jnp.maximum(jnp.sum((relation_ids == relation).astype(jnp.int32), axis=along), 1)
        for relation in range(RELATIONS)
    ]
    return jnp.stack(counted).astype(jnp.float32)


def first_means(columns, neighbours, relation_ids):
    dest_rows = neighbours.shape[1]
    picked = jnp.take(columns, neighbours, axis=1)
    counter = relation_counts(relation_ids, 0)
    slabs = [columns[:, :dest_rows]]
    for relation in range(RELATIONS):
        chosen = relation_ids == relation
        summed = jnp.sum(
            jnp.where(chosen[None], picked, jnp.zeros((), picked.dtype)), axis=1, dtype=jnp.float32
        )
        slabs.append((summed / counter[relation][None, :]).astype(jnp.bfloat16))
    return jnp.stack(slabs)


def place_requests(owner_flat, within_flat, batches, capacity):
    edges = owner_flat.shape[0]
    matches = (owner_flat[:, None] == jnp.arange(batches, dtype=jnp.int32)[None, :]).astype(
        jnp.bfloat16
    )
    order = jnp.arange(edges, dtype=jnp.int32)
    earlier = (order[None, :] < order[:, None]).astype(jnp.bfloat16)
    before = jnp.dot(earlier, matches, preferred_element_type=jnp.float32)
    slot_index = jnp.sum(before * matches.astype(jnp.float32), axis=1).astype(jnp.int32)
    places = (slot_index[:, None] == jnp.arange(capacity, dtype=jnp.int32)[None, :]).astype(
        jnp.float32
    )
    valued = matches.astype(jnp.float32) * within_flat.astype(jnp.float32)[:, None]
    request = jnp.einsum("eb,ec->bc", valued, places, precision=lax.Precision.HIGHEST).astype(
        jnp.int32
    )
    return (slot_index, request)


def body(feats, nbr_one, rel_one, w_one, owner_two, local_two, rel_two, w_two):
    columns = feats[0]
    slabs = first_means(columns, nbr_one[0], rel_one[0])
    batches = lax.axis_size("batch")
    capacity = (2 * ROWS * FANOUT_TWO + batches - 1) // batches
    span = batches * capacity
    labels = jnp.arange(RELATIONS * span, dtype=jnp.int32)
    owners = owner_two[0, :, :, 0]
    within = local_two[0]
    relation_ids = rel_two[0]
    portion = slabs
    hidden_one = jax.nn.relu(
        lax.psum_scatter(
            jnp.einsum("sfd,sfh->dh", portion, w_one, preferred_element_type=jnp.float32).astype(
                jnp.bfloat16
            ),
            "feat",
            scatter_dimension=0,
            tiled=True,
        ).astype(jnp.float32)
    ).astype(jnp.bfloat16)
    offset = lax.axis_index("feat") * ROWS
    mine_owner = lax.dynamic_slice_in_dim(owners, offset, ROWS, 0).reshape(-1)
    mine_within = lax.dynamic_slice_in_dim(within, offset, ROWS, 0).reshape(-1)
    mine_ids = lax.dynamic_slice_in_dim(relation_ids, offset, ROWS, 0)
    slot_index, request = place_requests(mine_owner, mine_within, batches, capacity)
    onehot = (
        lax.all_to_all(request, "batch", split_axis=0, concat_axis=0, tiled=True)[..., None]
        == jnp.arange(ROWS, dtype=jnp.int32)
    ).astype(jnp.bfloat16)
    replies = jnp.einsum(
        "bmr,rh->bmh", onehot, hidden_one, preferred_element_type=jnp.float32
    ).astype(jnp.bfloat16)
    arrived = lax.all_to_all(replies, "batch", split_axis=0, concat_axis=0, tiled=True)
    flat = arrived.reshape(span, arrived.shape[2])
    positions = (mine_owner * capacity + slot_index).reshape(ROWS, FANOUT_TWO)
    keys = mine_ids * span + positions
    table = jnp.zeros((ROWS, RELATIONS * span), jnp.bfloat16)
    for slot in range(FANOUT_TWO):
        table = table + (keys[:, slot][:, None] == labels[None, :]).astype(jnp.bfloat16)
    table = table.reshape(ROWS, RELATIONS, span)
    summed = jnp.einsum("drc,ch->rdh", table, flat, preferred_element_type=jnp.float32)
    counter = relation_counts(mine_ids, 1)
    means = (summed / counter[:, :, None]).astype(jnp.bfloat16)
    inputs = jnp.concatenate([hidden_one[None], means], axis=0)
    block_size = w_two.shape[1]
    shard_piece = lax.all_gather(w_two, "feat", axis=1, tiled=True)
    amount = shard_piece.shape[1]
    groups = amount // block_size
    portion = inputs
    portion = portion.reshape(portion.shape[0], portion.shape[1], groups, block_size)
    weights = shard_piece.reshape(shard_piece.shape[0], groups, block_size, shard_piece.shape[2])
    products = jnp.einsum("sdgk,sgkh->gdh", portion, weights, preferred_element_type=jnp.float32)
    rounded = lax.optimization_barrier(products.astype(jnp.bfloat16)).astype(jnp.float32)
    running = jnp.sum(rounded, axis=0)
    result = jax.nn.relu(running).astype(jnp.bfloat16)
    return result[None]


def solution(mesh):
    in_specs = (
        P("batch", "feat", None),
        P("batch", None, None),
        P("batch", None, None),
        P(None, "feat", None),
        P("batch", None, None, None),
        P("batch", None, None),
        P("batch", None, None),
        P(None, "feat", None),
    )
    out_specs = P("batch", "feat", None)
    return jax.shard_map(body, mesh=mesh, in_specs=in_specs, out_specs=out_specs, check_vma=False)
```

profile of v0, /device:TPU:1, one launch (start us, length us, event | category | flops | bytes accessed | tf_op | source)
XLA Modules:
  0.0 303.7 jit_solution(5919092703397115076)
XLA Ops:
  6.5 0.9 compare_select_fusion
  7.5 0.9 compare_and_fusion
  8.4 1.1 broadcast_compare_fusion.1
  9.4 1.1 convert_reduce_fusion.8
  10.6 2.0 copy.27
  12.6 0.9 fusion.45
  13.5 53.9 %gather_fusion = bf16[15360,48]{1,0:T(8,128)(2,1)} fusion(bf16[48,8192]{0,1:T(8,128)(2,1)S(1)} %copy.27, s32[15360]{0:T(1024)S(1)} %broadcast_clamp_fusion), kind=kCustom, calls=%fused_computation | custom fusion | bytes 3010560 | tf_op jit(solution)/shard_map/jit(_take)/gather | solution.py:21
  67.5 13.3 %convert_reduce_fusion = (f32[1024,48]{1,0:T(8,128)S(1)}, f32[1024,48]{1,0:T(8,128)S(1)}, f32[1024,48]{1,0:T(8,128)S(1)}, f32[1024,48]{1,0:T(8,128)S(1)}) fusion(pred[15,1024]{1,0:T(8,128)(4,1)S(1)} %get-tuple-element.41, bf16[15,1024,48]{2,1,0:T(8,128)(2,1)} %bitcast.106, pred[15,1024]{1,0:T(8,128)(4,1)S(1)} %compare_and_fusion, ...), kind=kLoop, calls=%fused_computation.3 | loop fusion | flops 9388032 | bytes 2337792 | tf_op jit(solution)/shard_map/reduce_sum | solution.py:26
  80.8 0.2 copy.28
  81.3 0.2 copy.30
  81.4 0.2 copy.31
  81.7 2.0 bitcast_convert_fusion.1
  83.9 0.7 all-gather.2.cloned.1.call-update
  84.6 0.8 constant_dynamic-slice_fusion.1
  85.6 0.3 fusion.11
  85.9 0.8 dynamic-slice_convert_fusion
  86.9 0.3 convolution_convert_fusion.1
  87.3 16.5 %all_to_all.14 = s32[32,1,40]{2,1,0:T(1,128)S(1)} all-to-all(s32[32,1,40]{2,1,0:T(1,128)S(1)} %bitcast.116), channel_id=1, replica_groups=mesh['feat'=16,'batch'=32] {'batch'}, dimensions={0} | all-to-all | bytes 10240 | tf_op jit(solution)/shard_map/all_to_all | solution.py:79
  103.8 48.4 %reduce-scatter.2.cloned.1.call-done = bf16[64,1024]{1,0:T(8,128)(2,1)} async-done(((bf16[1024,1024]{1,0:T(8,128)(2,1)}), bf16[64,1024]{1,0:T(8,128)(2,1)}) %reduce-scatter.2.cloned.1.call-update) | async-done | bytes 131088 | tf_op jit(solution)/shard_map/reduce_scatter | solution.py:64
  152.2 3.3 %convolution_convert_fusion = bf16[32,40,1024]{2,1,0:T(8,128)(2,1)} fusion(s32[32,40]{1,0:T(8,128)S(1)} %bitcast.111, bf16[64,1024]{1,0:T(8,128)(2,1)} %reduce-scatter.2.cloned.1.call-done), kind=kOutput, calls=%fused_computation.11 | convolution fusion | flops 169361408 | bytes 2757632 | tf_op jit(solution)/shard_map/bmr,rh->bmh/dot_general | solution.py:82
  155.5 18.1 %all-to-all-start.1 = ((bf16[32,40,1024]{2,1,0:T(8,128)(2,1)}), bf16[32,40,1024]{2,1,0:T(8,128)(2,1)S(1)}, u32[]{:S(2)}, u32[]{:S(2)}) async-start(bf16[32,40,1024]{2,1,0:T(8,128)(2,1)} %convolution_convert_fusion), calls=%async_computation.2 | async-start | bytes 5242880 | tf_op jit(solution)/shard_map/all_to_all | solution.py:85
  174.1 1.0 slice_reduce_fusion.9
  175.1 0.2 concatenate.12
  175.3 0.8 copy.36
  176.1 31.1 %all-to-all-done.1 = bf16[32,40,1024]{2,1,0:T(8,128)(2,1)S(1)} async-done(((bf16[32,40,1024]{2,1,0:T(8,128)(2,1)}), bf16[32,40,1024]{2,1,0:T(8,128)(2,1)S(1)}, u32[]{:S(2)}, u32[]{:S(2)}) %all-to-all-start.1) | async-done | bytes 2621472 | tf_op jit(solution)/shard_map/all_to_all | solution.py:85
  207.2 3.2 %fusion.9 = bf16[4,64,1024]{2,1,0:T(8,128)(2,1)} fusion(bf16[1280,1024,1]{1,0,2:T(8,128)(2,1)S(1)} %bitcast.107, s32[4,1280]{1,0:T(4,128)S(1)} %multiply_add_fusion, s32[64]{0:T(128)S(1)} %get-tuple-element.18, s32[64]{0:T(128)S(1)} %get-tuple-element.19, s32[64]{0:T(128)S(1)} %get-tuple-element.20, s32[64]{0:T(128)S(1)} %get-tuple-element.21, ...), kind=kOutput, calls=%fused_computation.29 | convolution fusion | flops 684720128 | bytes 3169792 | tf_op jit(solution)/shard_map/drc,ch->rdh/dot_general | solution.py:93
  210.3 1.8 concatenate.13
  212.2 0.3 copy.37
  212.4 77.0 %all-gather.2.cloned.1.call-done = bf16[5,1024,1024]{2,1,0:T(8,128)(2,1)} async-done(((bf16[5,64,1024]{2,1,0:T(8,128)(2,1)}), bf16[5,1024,1024]{2,1,0:T(8,128)(2,1)}) %all-gather.2.cloned.1.call-update) | async-done | bytes 10485776 | tf_op jit(solution)/shard_map/all_gather | solution.py:98
  289.4 6.3 %bitcast_convert_fusion = bf16[16,64,1024]{2,1,0:T(8,128)(2,1)S(1)} fusion(bf16[5,16,64,1024]{3,2,1,0:T(8,128)(2,1)} %bitcast.121, bf16[4,64,16,64]{3,1,0,2:T(8,128)(2,1)S(1)} %copy.37, bf16[1,64,16,64]{3,1,0,2:T(8,128)(2,1)S(1)} %copy-done.2), kind=kOutput, calls=%fused_computation.7 | convolution fusion | flops 672464896 | bytes 13238272 | tf_op jit(solution)/shard_map/sdgk,sgkh->gdh/dot_general | solution.py:104
  295.8 0.3 convert_reduce_fusion.4
  296.1 0.7 fusion.39
  (37 shorter events, 1.4 us)
Async XLA Ops:
  6.5 75.2 %copy-start = (bf16[5,48,1024]{2,1,0:T(8,128)(2,1)S(1)}, bf16[5,48,1024]{2,1,0:T(8,128)(2,1)}, u32[]{:S(2)}) copy-start(bf16[5,48,1024]{2,1,0:T(8,128)(2,1)} %param.11) | copy-start | bytes 1474564
  6.5 145.7 %reduce-scatter.2.cloned.1.call-start = ((), (), s32[]{:S(2)}) async-start(), calls=%async_computation.3 | async-start | bytes 2228224 | tf_op jit(solution)/shard_map/reduce_scatter | solution.py:64
  83.8 205.6 %all-gather.2.cloned.1.call-start = ((), (), s32[]{:S(2)}) async-start(), calls=%async_computation.4 | async-start | bytes 11141120 | tf_op jit(solution)/shard_map/all_gather | solution.py:98
  155.5 19.5 %copy-start.1 = (bf16[64,1024]{1,0:T(8,128)(2,1)S(1)}, bf16[64,1024]{1,0:T(8,128)(2,1)}, u32[]{:S(2)}) copy-start(bf16[64,1024]{1,0:T(8,128)(2,1)} %reduce-scatter.2.cloned.1.call-done) | copy-start | bytes 393220
  155.5 51.7 %all-to-all-start.1 = ((bf16[32,40,1024]{2,1,0:T(8,128)(2,1)}), bf16[32,40,1024]{2,1,0:T(8,128)(2,1)S(1)}, u32[]{:S(2)}, u32[]{:S(2)}) async-start(bf16[32,40,1024]{2,1,0:T(8,128)(2,1)} %convolution_convert_fusion), calls=%async_computation.2 | async-start | bytes 5242880 | tf_op jit(solution)/shard_map/all_to_all | solution.py:85
  210.3 79.1 %copy-start.2 = (bf16[1,64,16,64]{3,1,0,2:T(8,128)(2,1)S(1)}, bf16[1,64,16,64]{3,1,0,2:T(8,128)(2,1)}, u32[]{:S(2)}) copy-start(bf16[1,64,16,64]{3,1,0,2:T(8,128)(2,1)} %copy.36) | copy-start | bytes 393220
Sparse Core Ops, SparseCore 0:
  83.9 68.2 reduce-scatter.1
  154.3 135.1 all-gather.1
where the time goes:
time: 304 us
  waiting for transfers between devices  157 us (52%)
  local copies, waits for them, and re-layouts  63.1 us (21%)
  other arithmetic  19.5 us (6%)
  starting transfers between devices  18.1 us (6%)
  blocking collectives  16.5 us (5%)
  matrix products  15.5 us (5%)
  between operations  13.7 us (5%)
    all_gather x1, waiting for transfers between devices, body(): shard_piece = lax.all_gather(w_two, 'feat', axis=1, tiled=True)  77 us
    gather x1, local copies, waits for them, and re-layouts, first_means(): picked = jnp.take(columns, neighbours, axis=1)  53.9 us
    reduce_scatter x1, waiting for transfers between devices, body(): lax.psum_scatter(jnp.einsum('sfd,sfh->dh', portion, w_one, preferred_elem...  48.4 us
    all_to_all x1, waiting for transfers between devices, body(): lax.all_to_all(replies, 'batch', split_axis=0, concat_axis=0, tiled=True)  31.1 us
    all_to_all x1, starting transfers between devices, body(): lax.all_to_all(replies, 'batch', split_axis=0, concat_axis=0, tiled=True)  18.1 us
    all_to_all x1, blocking collectives, body(): lax.all_to_all(request, 'batch', split_axis=0, concat_axis=0, tiled=True)  16.5 us
    reduce_sum x1, other arithmetic, first_means(): jnp.sum(jnp.where(chosen[None], picked, jnp.zeros((), picked.dtype)), axi...  13.3 us
    dot_general x1, matrix products, body(): jnp.einsum('sdgk,sgkh->gdh', portion, weights, preferred_element_type=jnp...  6.34 us
  transfers between devices with their start and end apart: 3, of which 3 were waited for; matrix products, arithmetic and copies ran while one was open for 4% of the time, Pallas kernels for 0%

commit v1 on v0

--- a/solution.py
+++ b/solution.py
@@ -95,7 +95,9 @@
     means = (summed / counter[:, :, None]).astype(jnp.bfloat16)
     inputs = jnp.concatenate([hidden_one[None], means], axis=0)
     block_size = w_two.shape[1]
-    shard_piece = lax.all_gather(w_two, "feat", axis=1, tiled=True)
+    shard_piece = jnp.concatenate(
+        lax.all_to_all(jnp.stack([w_two] * lax.axis_size("feat")), "feat", 0, 0), axis=1
+    )
     amount = shard_piece.shape[1]
     groups = amount // block_size
     portion = inputs

time: 304 us -> 683 us (2.25)
  waiting for transfers between devices: 157 us -> 493 us
  blocking collectives: 16.5 us -> 68.6 us
  starting transfers between devices: 18.1 us -> 8.47 us
    all_to_all x1, waiting for transfers between devices: 31.1 us -> 444 us  [body(): lax.all_to_all(jnp.stack([w_two] * lax.axis_size('feat')), 'feat', 0, 0)]
    all_gather x1 -> x0, waiting for transfers between devices: 77 us -> none  [body(): shard_piece = lax.all_gather(w_two, 'feat', axis=1, tiled=True)]
    all_to_all x0 -> x1, blocking collectives: none -> 52 us  [body(): lax.all_to_all(replies, 'batch', split_axis=0, concat_axis=0, tiled=True)]
    all_to_all x1, starting transfers between devices: 18.1 us -> 8.47 us  [body(): lax.all_to_all(jnp.stack([w_two] * lax.axis_size('feat')), 'feat', 0, 0)]
  transfers between devices with their start and end apart: 3 -> 2, of which waited for: 3 -> 2; matrix products, arithmetic and copies ran while one was open for 4% -> 1% of each run, Pallas kernels for 0% -> 0%
where the time goes in v1:
time: 683 us; the launch traced here: 682 us
  waiting for transfers between devices  493 us (72%)
  local copies, waits for them, and re-layouts  68.6 us (10%)
  blocking collectives  68.6 us (10%)
  other arithmetic  16.2 us (2%)
  between operations  13.7 us (2%)
  matrix products  13.3 us (2%)
  starting transfers between devices  8.47 us (1%)
    all_to_all x1, waiting for transfers between devices, body(): lax.all_to_all(jnp.stack([w_two] * lax.axis_size('feat')), 'feat', 0, 0)  444 us
    gather x1, local copies, waits for them, and re-layouts, first_means(): picked = jnp.take(columns, neighbours, axis=1)  53.9 us
    all_to_all x1, blocking collectives, body(): lax.all_to_all(replies, 'batch', split_axis=0, concat_axis=0, tiled=True)  52 us
    reduce_scatter x1, waiting for transfers between devices, body(): lax.psum_scatter(jnp.einsum('sfd,sfh->dh', portion, w_one, preferred_elem...  49.1 us
    all_to_all x1, blocking collectives, body(): lax.all_to_all(request, 'batch', split_axis=0, concat_axis=0, tiled=True)  16.5 us
  transfers between devices with their start and end apart: 2, of which 2 were waited for; matrix products, arithmetic and copies ran while one was open for 1% of the time, Pallas kernels for 0%

profile of v1, /device:TPU:1, one launch (start us, length us, event | category | flops | bytes accessed | tf_op | source)
XLA Modules:
  0.0 682.1 jit_solution(4577967965146160522)
XLA Ops:
  6.5 1.0 fusion.45
  7.5 2.0 copy.25
  9.6 0.3 broadcast_compare_fusion.1
  9.9 0.3 convert_reduce_fusion.8
  10.2 53.9 %gather_fusion = bf16[15360,48]{1,0:T(8,128)(2,1)} fusion(bf16[48,8192]{0,1:T(8,128)(2,1)S(1)} %copy.25, s32[15360]{0:T(1024)S(1)} %broadcast_clamp_fusion), kind=kCustom, calls=%fused_computation | custom fusion | bytes 3010560 | tf_op jit(solution)/shard_map/jit(_take)/gather | solution.py:21
  64.2 13.3 %convert_reduce_fusion = (f32[1024,48]{1,0:T(8,128)S(1)}, f32[1024,48]{1,0:T(8,128)S(1)}, f32[1024,48]{1,0:T(8,128)S(1)}, f32[1024,48]{1,0:T(8,128)S(1)}) fusion(pred[15,1024]{1,0:T(8,128)(4,1)S(1)} %get-tuple-element.41, bf16[15,1024,48]{2,1,0:T(8,128)(2,1)} %bitcast.110, pred[15,1024]{1,0:T(8,128)(4,1)S(1)} %compare_and_fusion, ...), kind=kLoop, calls=%fused_computation.3 | loop fusion | flops 9388032 | bytes 2337792 | tf_op jit(solution)/shard_map/reduce_sum | solution.py:26
  77.6 0.2 copy.26
  77.8 0.2 copy.27
  78.0 0.2 copy.28
  78.2 0.2 copy.29
  78.5 2.1 bitcast_convert_fusion.1
  80.6 0.8 constant_dynamic-slice_fusion.1
  81.6 0.3 fusion.11
  81.9 0.8 dynamic-slice_convert_fusion
  83.0 0.3 convolution_convert_fusion.1
  83.3 16.5 %all_to_all.19 = s32[32,1,40]{2,1,0:T(1,128)S(1)} all-to-all(s32[32,1,40]{2,1,0:T(1,128)S(1)} %bitcast.120), channel_id=1, replica_groups=mesh['feat'=16,'batch'=32] {'batch'}, dimensions={0} | all-to-all | bytes 10240 | tf_op jit(solution)/shard_map/all_to_all | solution.py:79
  99.8 49.1 %reduce-scatter.2.cloned.1.call-done = bf16[64,1024]{1,0:T(8,128)(2,1)} async-done(((bf16[1024,1024]{1,0:T(8,128)(2,1)}), bf16[64,1024]{1,0:T(8,128)(2,1)}) %reduce-scatter.2.cloned.1.call-update) | async-done | bytes 131088 | tf_op jit(solution)/shard_map/reduce_scatter | solution.py:64
  148.9 1.8 convolution_convert_fusion
  150.7 52.0 %all_to_all.20 = bf16[32,40,1024]{2,1,0:T(8,128)(2,1)S(1)} all-to-all(bf16[32,40,1024]{2,1,0:T(8,128)(2,1)S(1)} %convolution_convert_fusion), channel_id=1, replica_groups=mesh['feat'=16,'batch'=32] {'batch'}, dimensions={0} | all-to-all | bytes 5242880 | tf_op jit(solution)/shard_map/all_to_all | solution.py:85
  202.8 5.2 stack.14
  208.0 8.5 %all-to-all-start.2 = ((bf16[16,5,64,1024]{3,2,1,0:T(8,128)(2,1)}), bf16[16,5,64,1024]{3,2,1,0:T(8,128)(2,1)}, u32[]{:S(2)}, u32[]{:S(2)}) async-start(bf16[16,5,64,1024]{3,2,1,0:T(8,128)(2,1)} %stack.14), calls=%async_computation.3 | async-start | bytes 20971520 | tf_op jit(solution)/shard_map/all_to_all | solution.py:99
  216.7 0.1 convert_reduce_fusion.12
  216.9 0.4 slice_reduce_fusion.9
  217.3 0.9 concatenate.12
  218.2 1.0 copy.34
  219.2 2.5 fusion.9
  221.7 1.8 concatenate.13
  223.5 0.3 copy.35
  223.7 444.2 %all-to-all-done.2 = bf16[16,5,64,1024]{3,2,1,0:T(8,128)(2,1)} async-done(((bf16[16,5,64,1024]{3,2,1,0:T(8,128)(2,1)}), bf16[16,5,64,1024]{3,2,1,0:T(8,128)(2,1)}, u32[]{:S(2)}, u32[]{:S(2)}) %all-to-all-start.2) | async-done | bytes 10485792 | tf_op jit(solution)/shard_map/all_to_all | solution.py:99
  667.9 6.3 bitcast_convert_fusion
  674.3 0.3 convert_reduce_fusion.4
  674.6 0.7 fusion.39
  (40 shorter events, 1.1 us)
Async XLA Ops:
  6.5 71.9 %copy-start = (bf16[5,48,1024]{2,1,0:T(8,128)(2,1)S(1)}, bf16[5,48,1024]{2,1,0:T(8,128)(2,1)}, u32[]{:S(2)}) copy-start(bf16[5,48,1024]{2,1,0:T(8,128)(2,1)} %param.11) | copy-start | bytes 1474564
  6.5 3.0 copy-start.4
  6.5 3.1 copy-start.3
  6.5 142.4 %reduce-scatter.2.cloned.1.call-start = ((), (), s32[]{:S(2)}) async-start(), calls=%async_computation.4 | async-start | bytes 2228224 | tf_op jit(solution)/shard_map/reduce_scatter | solution.py:64
  150.7 52.1 %copy-start.1 = (bf16[5,64,1024]{2,1,0:T(8,128)(2,1)S(1)}, bf16[5,64,1024]{2,1,0:T(8,128)(2,1)}, u32[]{:S(2)}) copy-start(bf16[5,64,1024]{2,1,0:T(8,128)(2,1)} %param.15) | copy-start | bytes 1966084
  208.0 9.3 %copy-start.2 = (bf16[64,1024]{1,0:T(8,128)(2,1)S(1)}, bf16[64,1024]{1,0:T(8,128)(2,1)}, u32[]{:S(2)}) copy-start(bf16[64,1024]{1,0:T(8,128)(2,1)} %reduce-scatter.2.cloned.1.call-done) | copy-start | bytes 393220
  208.0 459.9 %all-to-all-start.2 = ((bf16[16,5,64,1024]{3,2,1,0:T(8,128)(2,1)}), bf16[16,5,64,1024]{3,2,1,0:T(8,128)(2,1)}, u32[]{:S(2)}, u32[]{:S(2)}) async-start(bf16[16,5,64,1024]{3,2,1,0:T(8,128)(2,1)} %stack.14), calls=%async_computation.3 | async-start | bytes 20971520 | tf_op jit(solution)/shard_map/all_to_all | solution.py:99
Sparse Core Ops, SparseCore 0:
  80.7 68.1 reduce-scatter.1
